TPU v7x, 768 devices: a whole 4x8x12 slice. The times are simulated.
768 devices in a mesh: pair: 192 (over y, z, core), virt: 4 (over x).
Axes of the slice: x: 4, y: 8, z: 12, core: 2. Of those that a mesh axis runs over, the one named last changes fastest.
Arguments:
- amplitudes: bfloat16 [192, 4, 48, 128, 128], P('pair', 'virt'), may hold values from -6 to 6
- offsets: int32 [192, 4, 48, 1], P('pair', 'virt'), may hold values from 0 to 4; in each aligned block of 48 rows (0 to 47, 48 to 95, ..., all dimensions but the last counted through in order) at most 16 rows name the same one
- row_blocks: int32 [192, 4, 48], P('pair', 'virt'), may hold values from 0 to 3
- k_blocks: int32 [192, 4, 48], P('pair', 'virt'), may hold values from 0 to 7
- screen: int32 [192, 4, 48], P('pair', 'virt'), may hold values 0 or 1
- integrals: bfloat16 [192, 4096, 1024], P('pair', 'virt'), may hold values from -0.125 to 0.125
- row_gaps: float32 [98304], P('pair'), may hold values from 0.5 to 4
- col_gaps: float32 [1024], P('virt'), may hold values from 0.5 to 4
Outputs:
- update: float32 [98304, 1024], P('pair', 'virt')
Inputs may be any that keep to these rules, and one draw needn't show every extreme that they name: `offsets`: among the tiles of one device no offset value occurs more than 16 times, and some value reaches 16.
All inputs are finite; a program needn't handle non-finite values. No bound on the sum of `screen` on one device may be relied on, other than what follows from the above.
Results may differ from a plain program's by a relative error of at most 0.0025.
Values may be sent and summed in bfloat16 or wider, within the bound.
A program may use at most 32 MiB of HBM per device.

v0:
```python
import jax
import jax.numpy as jnp
from jax import lax
from jax.sharding import PartitionSpec as P

REACH = 2


def passed_along(x, axis, by):
    length = lax.axis_size(axis)
    return lax.ppermute(x, axis, [(i, (i + by) % length) for i in range(length)])


def on_device(amplitudes, offsets, row_blocks, k_blocks, screen, integrals, row_gaps, col_gaps):
    slot_count = amplitudes.shape[2]
    tile_edge = amplitudes.shape[3]
    k_count = integrals.shape[1] // tile_edge
    row_count = row_gaps.shape[0] // tile_edge
    tile_tags = jnp.stack([offsets[..., 0], row_blocks, k_blocks, screen], axis=-1)
    window_len = 2 * REACH + 1
    tile_parts = []
    tag_parts = []
    for source in range(window_len):
        if source == REACH:
            got_tiles, got_tags = (amplitudes, tile_tags)
        else:
            got_tiles, got_tags = passed_along((amplitudes, tile_tags), "pair", REACH - source)
        tile_parts.append(got_tiles)
        tag_parts.append(got_tags)
    near_tiles = jnp.concatenate(tile_parts, axis=0)
    near_tags = jnp.concatenate(tag_parts, axis=0)
    expected = (2 * REACH - jnp.arange(window_len, dtype=jnp.int32))[:, None, None]
    wanted = (near_tags[..., 0] == expected) & (near_tags[..., 3] == 1)
    cand_tiles = near_tiles.reshape(window_len * slot_count, tile_edge * tile_edge)
    cand_tags = near_tags.reshape(window_len * slot_count, 4)
    wanted = wanted.reshape(window_len * slot_count)
    block_index = cand_tags[:, 1] * k_count + cand_tags[:, 2]
    targets = jnp.arange(row_count * k_count, dtype=jnp.int32)[:, None]
    selector = ((block_index[None, :] == targets) & wanted[None, :]).astype(jnp.bfloat16)
    blocks = jnp.dot(selector, cand_tiles, preferred_element_type=jnp.float32).astype(jnp.bfloat16)
    assembled = blocks.reshape(row_count, k_count, tile_edge, tile_edge).transpose(0, 2, 1, 3)
    assembled = assembled.reshape(row_count * tile_edge, k_count * tile_edge)
    partial_value = jnp.dot(assembled, integrals[0], preferred_element_type=jnp.float32)
    cycle_term = lax.psum_scatter(partial_value, "virt", scatter_dimension=1, tiled=True)
    return cycle_term / (row_gaps[:, None] + col_gaps[None, :])


def solution(mesh):
    return jax.shard_map(
        on_device,
        mesh=mesh,
        in_specs=(
            P("pair", "virt", None, None, None),
            P("pair", "virt", None, None),
            P("pair", "virt", None),
            P("pair", "virt", None),
            P("pair", "virt", None),
            P("pair", "virt", None),
            P("pair"),
            P("virt"),
        ),
        out_specs=P("pair", "virt"),
        check_vma=False,
    )
```

profile of v0, /device:TPU:1, one launch (start us, length us, event | category | flops | bytes accessed | tf_op | source)
XLA Modules:
  0.0 147.5 jit_solution(14434438693958649251)
XLA Ops:
  6.5 0.0 copy-start
  6.5 0.0 reduce-scatter.2.cloned.1.call-start
  6.5 5.0 %collective-permute-start.4 = (bf16[1,1,48,128,128]{4,3,2,1,0:T(8,128)(2,1)}, bf16[1,1,48,128,128]{4,3,2,1,0:T(8,128)(2,1)}, u32[]{:S(2)}, u32[]{:S(2)}) collective-permute-start(bf16[1,1,48,128,128]{4,3,2,1,0:T(8,128)(2,1)} %param.8), channel_id=1, source_target_pairs={{0,8},{4,12},{8,16},{12,20},{16,24},{20,28},{24,32},{28,36},{32,40... | collective-permute-start | bytes 4718600 | tf_op jit(solution)/shard_map/ppermute | solution.py:11
  11.5 4.8 %collective-permute-start.5 = (bf16[1,1,48,128,128]{4,3,2,1,0:T(8,128)(2,1)}, bf16[1,1,48,128,128]{4,3,2,1,0:T(8,128)(2,1)}, u32[]{:S(2)}, u32[]{:S(2)}) collective-permute-start(bf16[1,1,48,128,128]{4,3,2,1,0:T(8,128)(2,1)} %param.8), channel_id=1, source_target_pairs={{0,4},{4,8},{8,12},{12,16},{16,20},{20,24},{24,28},{28,32},{32,36}... | collective-permute-start | bytes 4718600 | tf_op jit(solution)/shard_map/ppermute | solution.py:11
  16.4 6.6 %collective-permute-start.6 = (bf16[1,1,48,128,128]{4,3,2,1,0:T(8,128)(2,1)}, bf16[1,1,48,128,128]{4,3,2,1,0:T(8,128)(2,1)}, u32[]{:S(2)}, u32[]{:S(2)}) collective-permute-start(bf16[1,1,48,128,128]{4,3,2,1,0:T(8,128)(2,1)} %param.8), channel_id=1, source_target_pairs={{0,764},{4,0},{8,4},{12,8},{16,12},{20,16},{24,20},{28,24},{32,28}... | collective-permute-start | bytes 4718600 | tf_op jit(solution)/shard_map/ppermute | solution.py:11
  23.0 8.2 %collective-permute-start.7 = (bf16[1,1,48,128,128]{4,3,2,1,0:T(8,128)(2,1)}, bf16[1,1,48,128,128]{4,3,2,1,0:T(8,128)(2,1)}, u32[]{:S(2)}, u32[]{:S(2)}) collective-permute-start(bf16[1,1,48,128,128]{4,3,2,1,0:T(8,128)(2,1)} %param.8), channel_id=1, source_target_pairs={{0,760},{4,764},{8,0},{12,4},{16,8},{20,12},{24,16},{28,20},{32,24... | collective-permute-start | bytes 4718600 | tf_op jit(solution)/shard_map/ppermute | solution.py:11
  31.2 0.7 pad_add_fusion
  31.9 1.9 %collective-permute-start = (s32[1,1,48,4]{2,3,1,0:T(4,128)S(1)}, s32[1,1,48,4]{2,3,1,0:T(4,128)S(1)}, u32[]{:S(2)}, u32[]{:S(2)}) collective-permute-start(s32[1,1,48,4]{2,3,1,0:T(4,128)S(1)} %pad_add_fusion), channel_id=1, source_target_pairs={{0,8},{4,12},{8,16},{12,20},{16,24},{20,28},{24,32},{28,36},{32,40... | collective-permute-start | bytes 2312 | tf_op jit(solution)/shard_map/ppermute | solution.py:11
  33.8 0.1 broadcast_reduce_fusion
  33.9 0.1 eq.48
  34.0 42.9 %collective-permute-done = s32[1,1,48,4]{2,3,1,0:T(4,128)S(1)} collective-permute-done((s32[1,1,48,4]{2,3,1,0:T(4,128)S(1)}, s32[1,1,48,4]{2,3,1,0:T(4,128)S(1)}, u32[]{:S(2)}, u32[]{:S(2)}) %collective-permute-start) | collective-permute-done | bytes 800 | tf_op jit(solution)/shard_map/ppermute | solution.py:11
  76.8 1.9 %collective-permute-start.1 = (s32[1,1,48,4]{2,3,1,0:T(4,128)S(1)}, s32[1,1,48,4]{2,3,1,0:T(4,128)S(1)}, u32[]{:S(2)}, u32[]{:S(2)}) collective-permute-start(s32[1,1,48,4]{2,3,1,0:T(4,128)S(1)} %pad_add_fusion), channel_id=1, source_target_pairs={{0,4},{4,8},{8,12},{12,16},{16,20},{20,24},{24,28},{28,32},{32,36}... | collective-permute-start | bytes 2312 | tf_op jit(solution)/shard_map/ppermute | solution.py:11
  78.8 1.1 collective-permute-done.1
  79.9 3.9 %collective-permute-start.2 = (s32[1,1,48,4]{2,3,1,0:T(4,128)S(1)}, s32[1,1,48,4]{2,3,1,0:T(4,128)S(1)}, u32[]{:S(2)}, u32[]{:S(2)}) collective-permute-start(s32[1,1,48,4]{2,3,1,0:T(4,128)S(1)} %pad_add_fusion), channel_id=1, source_target_pairs={{0,764},{4,0},{8,4},{12,8},{16,12},{20,16},{24,20},{28,24},{32,28}... | collective-permute-start | bytes 2312 | tf_op jit(solution)/shard_map/ppermute | solution.py:11
  83.8 0.7 constant_dynamic-update-slice_fusion.2
  84.5 0.4 collective-permute-done.2
  84.9 6.7 %collective-permute-start.3 = (s32[1,1,48,4]{2,3,1,0:T(4,128)S(1)}, s32[1,1,48,4]{2,3,1,0:T(4,128)S(1)}, u32[]{:S(2)}, u32[]{:S(2)}) collective-permute-start(s32[1,1,48,4]{2,3,1,0:T(4,128)S(1)} %pad_add_fusion), channel_id=1, source_target_pairs={{0,760},{4,764},{8,0},{12,4},{16,8},{20,12},{24,16},{28,20},{32,24... | collective-permute-start | bytes 2312 | tf_op jit(solution)/shard_map/ppermute | solution.py:11
  91.6 0.7 collective-permute-done.3
  92.3 0.1 reshape.61
  92.4 0.1 eq.52
  92.5 0.1 squeeze.4
  92.6 0.0 collective-permute-done.4
  92.7 1.6 %constant_dynamic-update-slice_fusion.9 = bf16[5,1,48,128,128]{4,3,2,1,0:T(8,128)(2,1)S(1)} fusion(bf16[1,1,48,128,128]{4,3,2,1,0:T(8,128)(2,1)} %collective-permute-done.4), kind=kLoop, calls=%fused_computation.19 | loop fusion | bytes 3145728
  94.2 0.0 collective-permute-done.5
  94.2 1.7 %constant_dynamic-update-slice_fusion.8 = bf16[5,1,48,128,128]{4,3,2,1,0:T(8,128)(2,1)S(1)} fusion(bf16[5,1,48,128,128]{4,3,2,1,0:T(8,128)(2,1)S(1)} %constant_dynamic-update-slice_fusion.9, bf16[1,1,48,128,128]{4,3,2,1,0:T(8,128)(2,1)} %collective-permute-done.5), kind=kLoop, calls=%fused_computation.18 | loop fusion | bytes 3145728
  95.9 1.7 %constant_dynamic-update-slice_fusion.7 = bf16[5,1,48,128,128]{4,3,2,1,0:T(8,128)(2,1)S(1)} fusion(bf16[5,1,48,128,128]{4,3,2,1,0:T(8,128)(2,1)S(1)} %constant_dynamic-update-slice_fusion.8, bf16[1,1,48,128,128]{4,3,2,1,0:T(8,128)(2,1)} %param.8), kind=kLoop, calls=%fused_computation.17 | loop fusion | bytes 3145728
  97.6 0.0 collective-permute-done.6
  97.6 1.7 %constant_dynamic-update-slice_fusion.6 = bf16[5,1,48,128,128]{4,3,2,1,0:T(8,128)(2,1)S(1)} fusion(bf16[5,1,48,128,128]{4,3,2,1,0:T(8,128)(2,1)S(1)} %constant_dynamic-update-slice_fusion.7, bf16[1,1,48,128,128]{4,3,2,1,0:T(8,128)(2,1)} %collective-permute-done.6), kind=kLoop, calls=%fused_computation.16 | loop fusion | bytes 3145728
  99.3 0.0 collective-permute-done.7
  99.3 1.7 %constant_dynamic-update-slice_fusion.5 = bf16[5,1,48,128,128]{4,3,2,1,0:T(8,128)(2,1)S(1)} fusion(bf16[5,1,48,128,128]{4,3,2,1,0:T(8,128)(2,1)S(1)} %constant_dynamic-update-slice_fusion.6, bf16[1,1,48,128,128]{4,3,2,1,0:T(8,128)(2,1)} %collective-permute-done.7), kind=kLoop, calls=%fused_computation.15 | loop fusion | bytes 3145728 | tf_op jit(solution)/shard_map/concatenate | solution.py:30
  101.0 0.0 copy-start.1
  101.0 0.0 copy-start.2
  101.1 4.5 %convolution_convert_fusion = bf16[32,16384]{1,0:T(8,128)(2,1)S(1)} fusion(bf16[30,8,128,128]{3,2,1,0:T(8,128)(2,1)S(1)} %bitcast.22, s32[240]{0:T(256)S(1)} %bitcast.24, pred[240]{0:T(512)(128)(4,1)S(1)} %compare_and_fusion), kind=kOutput, calls=%fused_computation | convolution fusion | flops 252197888 | bytes 8914096 | tf_op jit(solution)/shard_map/dot_general | solution.py:40
  105.5 0.0 copy-done
  105.5 2.6 %fusion.2 = f32[512,1024]{1,0:T(8,128)} fusion(bf16[1,1024,1024]{2,1,0:T(8,128)(2,1)S(1)} %copy-done, bf16[64,8,8,128]{3,2,1,0:T(8,128)(2,1)S(1)} %bitcast.23), kind=kOutput, calls=%fused_computation.3 | convolution fusion | flops 1073741824 | bytes 5242880 | tf_op jit(solution)/shard_map/dot_general | solution.py:43
  108.1 0.0 reduce-scatter.2.cloned.1.call-update
  108.1 30.5 %reduce-scatter.2.cloned.1.call-done = f32[512,256]{1,0:T(8,128)} async-done(((f32[512,1024]{1,0:T(8,128)}), f32[512,256]{1,0:T(8,128)}) %reduce-scatter.2.cloned.1.call-update) | async-done | bytes 524304 | tf_op jit(solution)/shard_map/reduce_scatter | solution.py:44
  138.6 0.0 copy-done.1
  138.6 0.0 copy-done.2
  138.6 2.0 %add_divide_fusion = f32[512,256]{1,0:T(8,128)} fusion(f32[512,256]{1,0:T(8,128)} %reduce-scatter.2.cloned.1.call-done, f32[256]{0:T(256)S(1)} %copy-done.2, f32[512]{0:T(512)S(1)} %copy-done.1), kind=kLoop, calls=%fused_computation.7 | loop fusion | flops 262144 | bytes 1051648 | tf_op jit(solution)/shard_map/div | solution.py:45
  (10 shorter events, 0.1 us)
Async XLA Ops:
  6.5 99.0 %copy-start = (bf16[1,1024,1024]{2,1,0:T(8,128)(2,1)S(1)}, bf16[1,1024,1024]{2,1,0:T(8,128)(2,1)}, u32[]{:S(2)}) copy-start(bf16[1,1024,1024]{2,1,0:T(8,128)(2,1)} %param.13) | copy-start | bytes 6291460
  6.5 132.1 %reduce-scatter.2.cloned.1.call-start = ((), (), s32[]{:S(2)}) async-start(), calls=%async_computation.1 | async-start | bytes 2621440 | tf_op jit(solution)/shard_map/reduce_scatter | solution.py:44
  6.5 86.1 %collective-permute-start.4 = (bf16[1,1,48,128,128]{4,3,2,1,0:T(8,128)(2,1)}, bf16[1,1,48,128,128]{4,3,2,1,0:T(8,128)(2,1)}, u32[]{:S(2)}, u32[]{:S(2)}) collective-permute-start(bf16[1,1,48,128,128]{4,3,2,1,0:T(8,128)(2,1)} %param.8), channel_id=1, source_target_pairs={{0,8},{4,12},{8,16},{12,20},{16,24},{20,28},{24,32},{28,36},{32,40... | collective-permute-start | bytes 4718600 | tf_op jit(solution)/shard_map/ppermute | solution.py:11
  11.5 82.7 %collective-permute-start.5 = (bf16[1,1,48,128,128]{4,3,2,1,0:T(8,128)(2,1)}, bf16[1,1,48,128,128]{4,3,2,1,0:T(8,128)(2,1)}, u32[]{:S(2)}, u32[]{:S(2)}) collective-permute-start(bf16[1,1,48,128,128]{4,3,2,1,0:T(8,128)(2,1)} %param.8), channel_id=1, source_target_pairs={{0,4},{4,8},{8,12},{12,16},{16,20},{20,24},{24,28},{28,32},{32,36}... | collective-permute-start | bytes 4718600 | tf_op jit(solution)/shard_map/ppermute | solution.py:11
  16.4 81.3 %collective-permute-start.6 = (bf16[1,1,48,128,128]{4,3,2,1,0:T(8,128)(2,1)}, bf16[1,1,48,128,128]{4,3,2,1,0:T(8,128)(2,1)}, u32[]{:S(2)}, u32[]{:S(2)}) collective-permute-start(bf16[1,1,48,128,128]{4,3,2,1,0:T(8,128)(2,1)} %param.8), channel_id=1, source_target_pairs={{0,764},{4,0},{8,4},{12,8},{16,12},{20,16},{24,20},{28,24},{32,28}... | collective-permute-start | bytes 4718600 | tf_op jit(solution)/shard_map/ppermute | solution.py:11
  23.0 76.4 %collective-permute-start.7 = (bf16[1,1,48,128,128]{4,3,2,1,0:T(8,128)(2,1)}, bf16[1,1,48,128,128]{4,3,2,1,0:T(8,128)(2,1)}, u32[]{:S(2)}, u32[]{:S(2)}) collective-permute-start(bf16[1,1,48,128,128]{4,3,2,1,0:T(8,128)(2,1)} %param.8), channel_id=1, source_target_pairs={{0,760},{4,764},{8,0},{12,4},{16,8},{20,12},{24,16},{28,20},{32,24... | collective-permute-start | bytes 4718600 | tf_op jit(solution)/shard_map/ppermute | solution.py:11
  31.9 45.0 %collective-permute-start = (s32[1,1,48,4]{2,3,1,0:T(4,128)S(1)}, s32[1,1,48,4]{2,3,1,0:T(4,128)S(1)}, u32[]{:S(2)}, u32[]{:S(2)}) collective-permute-start(s32[1,1,48,4]{2,3,1,0:T(4,128)S(1)} %pad_add_fusion), channel_id=1, source_target_pairs={{0,8},{4,12},{8,16},{12,20},{16,24},{20,28},{24,32},{28,36},{32,40... | collective-permute-start | bytes 2312 | tf_op jit(solution)/shard_map/ppermute | solution.py:11
  76.8 3.0 %collective-permute-start.1 = (s32[1,1,48,4]{2,3,1,0:T(4,128)S(1)}, s32[1,1,48,4]{2,3,1,0:T(4,128)S(1)}, u32[]{:S(2)}, u32[]{:S(2)}) collective-permute-start(s32[1,1,48,4]{2,3,1,0:T(4,128)S(1)} %pad_add_fusion), channel_id=1, source_target_pairs={{0,4},{4,8},{8,12},{12,16},{16,20},{20,24},{24,28},{28,32},{32,36}... | collective-permute-start | bytes 2312 | tf_op jit(solution)/shard_map/ppermute | solution.py:11
  79.9 5.0 %collective-permute-start.2 = (s32[1,1,48,4]{2,3,1,0:T(4,128)S(1)}, s32[1,1,48,4]{2,3,1,0:T(4,128)S(1)}, u32[]{:S(2)}, u32[]{:S(2)}) collective-permute-start(s32[1,1,48,4]{2,3,1,0:T(4,128)S(1)} %pad_add_fusion), channel_id=1, source_target_pairs={{0,764},{4,0},{8,4},{12,8},{16,12},{20,16},{24,20},{28,24},{32,28}... | collective-permute-start | bytes 2312 | tf_op jit(solution)/shard_map/ppermute | solution.py:11
  84.9 7.4 %collective-permute-start.3 = (s32[1,1,48,4]{2,3,1,0:T(4,128)S(1)}, s32[1,1,48,4]{2,3,1,0:T(4,128)S(1)}, u32[]{:S(2)}, u32[]{:S(2)}) collective-permute-start(s32[1,1,48,4]{2,3,1,0:T(4,128)S(1)} %pad_add_fusion), channel_id=1, source_target_pairs={{0,760},{4,764},{8,0},{12,4},{16,8},{20,12},{24,16},{28,20},{32,24... | collective-permute-start | bytes 2312 | tf_op jit(solution)/shard_map/ppermute | solution.py:11
  101.0 37.6 %copy-start.1 = (f32[512]{0:T(512)S(1)}, f32[512]{0:T(512)}, u32[]{:S(2)}) copy-start(f32[512]{0:T(512)} %param.14) | copy-start | bytes 6148
  101.0 37.6 %copy-start.2 = (f32[256]{0:T(256)S(1)}, f32[256]{0:T(256)}, u32[]{:S(2)}) copy-start(f32[256]{0:T(256)} %param.15) | copy-start | bytes 3076
Sparse Core Ops, SparseCore 0:
  108.3 30.3 reduce-scatter.1
where the time goes:
time: 148 us; the launch traced here: 147 us
  waiting for transfers between devices  75.6 us (51%)
  starting transfers between devices  39 us (26%)
  between operations  13.6 us (9%)
  local copies, waits for them, and re-layouts  8.78 us (6%)
  matrix products  7.04 us (5%)
  other arithmetic  3.46 us (2%)
    ppermute x8, waiting for transfers between devices, passed_along(): lax.ppermute(x, axis, [(i, (i + by) % length) for i in range(length)])  45.1 us
    ppermute x8, starting transfers between devices, passed_along(): lax.ppermute(x, axis, [(i, (i + by) % length) for i in range(length)])  39 us
    reduce_scatter x1, waiting for transfers between devices, on_device(): lax.psum_scatter(partial_value, 'virt', scatter_dimension=1, tiled=True)  30.5 us
    unnamed x13, local copies, waits for them, and re-layouts  6.66 us
    dot_general x1, matrix products, on_device(): jnp.dot(selector, cand_tiles, preferred_element_type=jnp.float32)  4.45 us
  transfers between devices with their start and end apart: 9, of which 5 were waited for; matrix products, arithmetic and copies ran while one was open for 6% of the time, Pallas kernels for 0%

commit v1 on v0

v1 whole, which is shorter than its diff:
```python
import functools
import jax
import jax.numpy as jnp
from jax import lax
from jax.experimental import pallas as pl
from jax.experimental.pallas import tpu as pltpu
from jax.sharding import PartitionSpec as P

REACH = 2
WINDOW = 2 * REACH + 1
CAP = 16
CANDS = WINDOW * CAP
LANES = 128
CHUNKS = 4
MESH = pl.DeviceIdType.MESH
PEERS = (4, 3, 1, 0)


def kernel(n_pair, n_virt, row_count, k_count, idx_ref, tag_ref, amp_hbm, int_hbm, out_ref,
           amps_recv, ints, pack, pref, assembled, tags_in, order, order_s, own, xsend, xrecv,
           amp_sem, int_sem, order_sem, tag_send, tag_recv, tile_send, tile_recv, x_send, x_recv):
    p = lax.axis_index("pair")
    v = lax.axis_index("virt")
    amps, recv = amps_recv
    rows, edge = recv[0].shape[1:]
    cols = out_ref.shape[1]
    pair_of = [lax.rem(p + o - REACH + n_pair, n_pair) for o in range(WINDOW)]
    virt_of = [lax.rem(v + t, n_virt) for t in range(n_virt)]

    barrier = pltpu.get_barrier_semaphore()
    for o in PEERS:
        pl.semaphore_signal(barrier, inc=1, device_id=(pair_of[o], v), device_id_type=MESH)
    for t in range(1, n_virt):
        pl.semaphore_signal(barrier, inc=1, device_id=(p, virt_of[t]), device_id_type=MESH)

    amp_copies = []
    for j in range(CHUNKS):
        c = pltpu.make_async_copy(amp_hbm.at[0, 0, :, pl.ds(j * rows, rows), :], amps[j], amp_sem.at[j])
        c.start()
        amp_copies.append(c)
    send_order = (2, 1, 3, 0)
    int_copies = {}
    for t in send_order:
        start = pl.multiple_of(virt_of[t] * cols, cols)
        c = pltpu.make_async_copy(int_hbm.at[0, :, pl.ds(start, cols)], ints.at[t], int_sem.at[t])
        c.start()
        int_copies[t] = c

    def pack_chunk(j):
        for o in PEERS + (REACH,):
            def body(s, _, o=o):
                tile = amps[j][jnp.clip(idx_ref[o * CAP + s], 0, amps[j].shape[0] - 1)]
                if o == REACH:
                    recv[j][o * CAP + s] = tile
                else:
                    pack[j, o, s] = tile
                return 0
            lax.fori_loop(0, CAP, body, 0, unroll=True)

    tile_copies = {}

    def send_chunk(j):
        for o in PEERS:
            c = pltpu.make_async_remote_copy(
                src_ref=pack.at[j, o], dst_ref=recv[j].at[pl.ds(o * CAP, CAP)],
                send_sem=tile_send.at[j, o], recv_sem=tile_recv.at[j, o],
                device_id=(pair_of[o], v), device_id_type=MESH)
            c.start()
            tile_copies[j, o] = c

    amp_copies[0].wait()
    pack_chunk(0)
    pl.semaphore_wait(barrier, len(PEERS) + n_virt - 1)
    tag_copies = []
    for o in PEERS:
        c = pltpu.make_async_remote_copy(
            src_ref=tag_ref, dst_ref=tags_in.at[o], send_sem=tag_send.at[o], recv_sem=tag_recv.at[o],
            device_id=(pair_of[o], v), device_id_type=MESH)
        c.start()
        tag_copies.append(c)
    send_chunk(0)
    for j in range(1, CHUNKS):
        amp_copies[j].wait()
        pack_chunk(j)
        send_chunk(j)

    for c in tag_copies:
        c.wait()
    lane8 = lax.broadcasted_iota(jnp.int32, (8, LANES), 1)
    tag8 = jnp.full((8, LANES), row_count * k_count, jnp.int32)
    for o in range(WINDOW):
        got = tag_ref[...] if o == REACH else tags_in[o]
        tag8 = jnp.where((lane8 >= o * CAP) & (lane8 < (o + 1) * CAP), got, tag8)
    lane = lax.broadcasted_iota(jnp.int32, (LANES, LANES), 1).astype(jnp.float32)
    sub = lax.broadcasted_iota(jnp.int32, (LANES, LANES), 0).astype(jnp.float32)
    tag_r = jnp.broadcast_to(tag8[0:1, :].astype(jnp.float32), (LANES, LANES))
    tag_c = tag_r.T
    key_r = tag_r * LANES + lane
    key_c = tag_c * LANES + sub
    rank_c = jnp.sum(jnp.where(key_r < key_c, 1.0, 0.0), axis=1, keepdims=True)
    again_c = jnp.max(jnp.where((tag_r == tag_c) & (lane < sub), 1.0, 0.0), axis=1, keepdims=True)
    here = jnp.where(rank_c == lane, 1.0, 0.0)
    perm = jnp.sum(here * sub, axis=0, keepdims=True)
    again = jnp.sum(here * again_c, axis=0, keepdims=True)
    upto = jnp.sum(jnp.where(tag_c <= lane, 1.0, 0.0), axis=0, keepdims=True)
    equal = jnp.sum(jnp.where(tag_c == lane, 1.0, 0.0), axis=0, keepdims=True)
    last = jnp.where(equal > 0, upto - 1.0, float(CANDS))
    order[...] = jnp.zeros_like(order)
    order[0:1, :] = perm.astype(jnp.int32)
    order[1:2, :] = again.astype(jnp.int32)
    order[2:3, :] = last.astype(jnp.int32)
    to_scalar = pltpu.make_async_copy(order, order_s, order_sem)
    to_scalar.start()
    pref[CANDS] = jnp.zeros_like(pref[CANDS])
    to_scalar.wait()

    x_copies = {}

    def finish(j):
        for t in range(1, n_virt):
            x_copies[j, t].wait()
        total = own[j % 2]
        for t in range(1, n_virt):
            total = total + xrecv[j, t].astype(jnp.float32)
        for r in range(row_count):
            out_ref[pl.ds(r * edge + j * rows, rows), :] = total[r * rows:(r + 1) * rows]

    for j in range(CHUNKS):
        for o in PEERS:
            tile_copies[j, o].wait()

        def add(i, acc, j=j):
            for u in range(8):
                at = i * 8 + u
                tile = recv[j][jnp.clip(order_s[0, at], 0, CANDS - 1)].astype(jnp.float32)
                acc = acc * order_s[1, at].astype(jnp.float32) + tile
                pref[at] = acc.astype(jnp.bfloat16)
            return acc

        lax.fori_loop(0, CANDS // 8, add, jnp.zeros((rows, LANES), jnp.float32))
        for r in range(row_count):
            for k in range(k_count):
                assembled[pl.ds(r * rows, rows), pl.ds(k * LANES, LANES)] = pref[jnp.clip(order_s[2, r * k_count + k], 0, CANDS)]
        for t in send_order:
            if j == 0:
                int_copies[t].wait()
            part = jnp.dot(assembled[...], ints[t], preferred_element_type=jnp.float32)
            if t == 0:
                own[j % 2] = part
            else:
                xsend[j, t] = part.astype(jnp.bfloat16)
                c = pltpu.make_async_remote_copy(
                    src_ref=xsend.at[j, t], dst_ref=xrecv.at[j, t], send_sem=x_send.at[j, t], recv_sem=x_recv.at[j, t],
                    device_id=(p, virt_of[t]), device_id_type=MESH)
                c.start()
                x_copies[j, t] = c
        if j > 0:
            finish(j - 1)
    finish(CHUNKS - 1)


def on_device(n_pair, n_virt, amplitudes, offsets, row_blocks, k_blocks, screen, integrals, row_gaps, col_gaps):
    slots, edge = amplitudes.shape[2], amplitudes.shape[3]
    k_count = integrals.shape[1] // edge
    row_count = row_gaps.shape[0] // edge
    cols = col_gaps.shape[0]
    rows = edge // CHUNKS
    off, blk = offsets[0, 0, :, 0], row_blocks[0, 0] * k_count + k_blocks[0, 0]
    wanted = jnp.where(screen[0, 0] == 1, off, -1)
    slot = jnp.arange(slots, dtype=jnp.int32)
    earlier = (wanted[:, None] == wanted[None, :]) & (slot[:, None] < slot[None, :])
    rank = jnp.sum(earlier.astype(jnp.int32), axis=0)
    place = jnp.where(wanted < 0, -1, wanted * CAP + rank)
    lane = jnp.arange(LANES, dtype=jnp.int32)
    hit = place[None, :] == lane[:, None]
    idx = jnp.sum(jnp.where(hit, slot[None, :], 0), axis=1)
    none = row_count * k_count
    tag = none + jnp.sum(jnp.where(hit, blk[None, :] - none, 0), axis=1)
    tag = jnp.broadcast_to(tag[None, :], (8, LANES))

    cycle = pl.pallas_call(
        functools.partial(kernel, n_pair, n_virt, row_count, k_count),
        out_shape=jax.ShapeDtypeStruct((row_count * edge, cols), jnp.float32),
        in_specs=[
            pl.BlockSpec(memory_space=pltpu.SMEM),
            pl.BlockSpec(memory_space=pltpu.VMEM),
            pl.BlockSpec(memory_space=pl.ANY),
            pl.BlockSpec(memory_space=pl.ANY),
        ],
        out_specs=pl.BlockSpec(memory_space=pltpu.VMEM),
        scratch_shapes=[
            ([pltpu.VMEM((slots, rows, edge), jnp.bfloat16)] * CHUNKS, [pltpu.VMEM((CANDS, rows, edge), jnp.bfloat16)] * CHUNKS),
            pltpu.VMEM((n_virt, k_count * edge, cols), jnp.bfloat16),
            pltpu.VMEM((CHUNKS, WINDOW, CAP, rows, edge), jnp.bfloat16),
            pltpu.VMEM((CANDS + 1, rows, edge), jnp.bfloat16),
            pltpu.VMEM((row_count * rows, k_count * edge), jnp.bfloat16),
            pltpu.VMEM((WINDOW, 8, LANES), jnp.int32),
            pltpu.VMEM((8, LANES), jnp.int32),
            pltpu.SMEM((8, LANES), jnp.int32),
            pltpu.VMEM((2, row_count * rows, cols), jnp.float32),
            pltpu.VMEM((CHUNKS, n_virt, row_count * rows, cols), jnp.bfloat16),
            pltpu.VMEM((CHUNKS, n_virt, row_count * rows, cols), jnp.bfloat16),
            pltpu.SemaphoreType.DMA((CHUNKS,)),
            pltpu.SemaphoreType.DMA((n_virt,)),
            pltpu.SemaphoreType.DMA,
            pltpu.SemaphoreType.DMA((WINDOW,)),
            pltpu.SemaphoreType.DMA((WINDOW,)),
            pltpu.SemaphoreType.DMA((CHUNKS, WINDOW)),
            pltpu.SemaphoreType.DMA((CHUNKS, WINDOW)),
            pltpu.SemaphoreType.DMA((CHUNKS, n_virt)),
            pltpu.SemaphoreType.DMA((CHUNKS, n_virt)),
        ],
        compiler_params=pltpu.CompilerParams(
            collective_id=0, has_side_effects=True, vmem_limit_bytes=60 * 1024 * 1024),
        name="cycle",
    )(idx, tag, amplitudes, integrals)
    return cycle / (row_gaps[:, None] + col_gaps[None, :])


def solution(mesh):
    return jax.shard_map(
        functools.partial(on_device, mesh.shape["pair"], mesh.shape["virt"]),
        mesh=mesh,
        in_specs=(
            P("pair", "virt", None, None, None),
            P("pair", "virt", None, None),
            P("pair", "virt", None),
            P("pair", "virt", None),
            P("pair", "virt", None),
            P("pair", "virt", None),
            P("pair"),
            P("virt"),
        ),
        out_specs=P("pair", "virt"),
        check_vma=False,
    )
```

time: 148 us -> 48.9 us (0.33)
  waiting for transfers between devices: 75.6 us -> 0 us
  Pallas kernels: 0 us -> 43.9 us
  starting transfers between devices: 39 us -> 0 us
  between operations: 13.6 us -> 0.03 us
  local copies, waits for them, and re-layouts: 8.78 us -> 0.6 us
  matrix products: 7.04 us -> 0 us
    ppermute x8 -> x0, waiting for transfers between devices: 45.1 us -> none  [passed_along(): lax.ppermute(x, axis, [(i, (i + by) % length) for i in range(length)])]
    pallas_call x0 -> x1, Pallas kernels: none -> 43.9 us  [on_device(): pl.pallas_call(functools.partial(kernel, n_pair, n_virt, row_count, k_cou...]
    ppermute x8 -> x0, starting transfers between devices: 39 us -> none  [passed_along(): lax.ppermute(x, axis, [(i, (i + by) % length) for i in range(length)])]
    reduce_scatter x1 -> x0, waiting for transfers between devices: 30.5 us -> none  [on_device(): lax.psum_scatter(partial_value, 'virt', scatter_dimension=1, tiled=True)]
    dot_general x2 -> x0, matrix products: 7.04 us -> none  [the longest x1 4.45 us: on_device(): jnp.dot(selector, cand_tiles, preferred_element_type=jnp.float32)]
    unnamed x13 -> x4, local copies, waits for them, and re-layouts: 6.66 us -> 0.01 us
    concatenate x3 -> x0, local copies, waits for them, and re-layouts: 1.7 us -> none  [the longest x1 1.68 us: on_device(): near_tiles = jnp.concatenate(tile_parts, axis=0)]
  transfers between devices with their start and end apart: 9 -> 0, of which waited for: 5 -> 0; matrix products, arithmetic and copies ran while one was open for 6% -> 0% of each run, Pallas kernels for 0% -> 0%
where the time goes in v1:
time: 48.9 us; the launch traced here: 48.7 us
  Pallas kernels  43.9 us (90%)
  other arithmetic  4.12 us (8%)
  local copies, waits for them, and re-layouts  0.6 us (1%)
    pallas_call x1, Pallas kernels, on_device(): pl.pallas_call(functools.partial(kernel, n_pair, n_virt, row_count, k_cou...  43.9 us
    div x1, other arithmetic, on_device(): return cycle / (row_gaps[:, None] + col_gaps[None, :])  1.98 us

profile of v1, /device:TPU:1, one launch (start us, length us, event | category | flops | bytes accessed | tf_op | source)
XLA Modules:
  0.0 48.7 jit_solution(6279794132882816622)
XLA Ops:
  0.0 0.7 %bitcast_select_fusion = s32[48]{0:T(128)S(1)} fusion(s32[1,1,48]{2,1,0:T(1,128)} %param.12, s32[1,1,48,1]{2,3,1,0:T(1,128)} %param.9), kind=kLoop, calls=%fused_computation.7 | loop fusion | flops 96 | bytes 576 | tf_op jit(solution)/shard_map/jit(_where)/select_n | solution.py:169
  0.7 0.1 convert_reduce_fusion
  0.8 0.7 %add_bitcast_fusion = s32[48]{0:T(128)S(1)} fusion(s32[1,1,48]{2,1,0:T(1,128)} %param.11, s32[1,1,48]{2,1,0:T(1,128)} %param.10), kind=kLoop, calls=%fused_computation.9 | loop fusion | flops 144 | bytes 576 | tf_op jit(solution)/shard_map/sub | solution.py:178
  1.5 0.7 %select_reduce_fusion = (s32[128]{0:T(128)S(1)}, s32[128]{0:T(128)}) fusion(s32[48]{0:T(128)S(1)} %add_bitcast_fusion, s32[48]{0:T(128)S(1)} %compare_select_fusion), kind=kLoop, calls=%fused_computation.1 | loop fusion | flops 30464 | bytes 1408 | tf_op jit(solution)/shard_map/reduce_sum | solution.py:178
  2.1 0.6 %broadcast_in_dim.44.tag_ref = s32[8,128]{1,0:T(8,128)} broadcast(s32[128]{0:T(128)S(1)} %broadcast_add_fusion), dimensions={1} | broadcast | bytes 4608 | tf_op jit(solution)/shard_map/broadcast_in_dim | solution.py:179
  2.7 0.0 copy-start
  2.7 0.0 copy-start.1
  2.7 43.9 %cycle.1 = f32[512,256]{1,0:T(8,128)} custom-call(s32[128]{0:T(128)} %get-tuple-element.6.idx_ref, s32[8,128]{1,0:T(8,128)} %broadcast_in_dim.44.tag_ref, bf16[1,1,48,128,128]{4,3,2,1,0:T(8,128)(2,1)} %amp_hbm.1, bf16[1,1024,1024]{2,1,0:T(8,128)(2,1)} %int_hbm.1), custom_call_target="tpu_custom_call" | custom-call | tf_op jit(solution)/shard_map/cycle/pallas_call | solution.py:181
  46.7 0.0 copy-done
  46.7 0.0 copy-done.1
  46.7 2.0 %add_divide_fusion = f32[512,256]{1,0:T(8,128)} fusion(f32[512,256]{1,0:T(8,128)} %cycle.1, f32[256]{0:T(256)S(1)} %copy-done.1, f32[512]{0:T(512)S(1)} %copy-done), kind=kLoop, calls=%fused_computation | loop fusion | flops 262144 | bytes 1051648 | tf_op jit(solution)/shard_map/div | solution.py:217
  (2 shorter events, 0.0 us)
Async XLA Ops:
  2.7 44.0 %copy-start = (f32[512]{0:T(512)S(1)}, f32[512]{0:T(512)}, u32[]{:S(2)}) copy-start(f32[512]{0:T(512)} %param.14) | copy-start | bytes 6148
  2.7 44.0 %copy-start.1 = (f32[256]{0:T(256)S(1)}, f32[256]{0:T(256)}, u32[]{:S(2)}) copy-start(f32[256]{0:T(256)} %param.15) | copy-start | bytes 3076

commit v2 on v1

v2 whole, which is shorter than its diff:
```python
import functools
import jax
import jax.numpy as jnp
from jax import lax
from jax.experimental import pallas as pl
from jax.experimental.pallas import tpu as pltpu
from jax.sharding import PartitionSpec as P

REACH = 2
WINDOW = 2 * REACH + 1
CAP = 16
CANDS = WINDOW * CAP
LANES = 128
SIZES = (32, 32, 32, 16, 16)
STARTS = tuple(sum(SIZES[:j]) for j in range(len(SIZES)))
CHUNKS = len(SIZES)
AHEAD = 3
LAG = 2
MESH = pl.DeviceIdType.MESH
PEERS = (4, 3, 1, 0)


def kernel(n_pair, n_virt, row_count, k_count, off_hbm, row_hbm, kb_hbm, screen_hbm, amp_hbm, int_hbm, rgap_hbm, cgap_hbm, out_ref,
           amps, pack, recv, pref, assembled, own, xsend, xrecv, ints, tags_in, tag_own, rowbuf, small, rgap, cgap, rowmat, order, idx_s, order_s,
           amp_sem, int_sem, small_sem, gap_sem, idx_sem, order_sem, tag_send, tag_recv, tile_send, tile_recv, x_send, x_recv):
    p = lax.axis_index("pair")
    v = lax.axis_index("virt")
    slots, edge = amp_hbm.shape[2:4]
    cols = out_ref.shape[1]
    pair_of = [lax.rem(p + o - REACH + n_pair, n_pair) for o in range(WINDOW)]
    virt_of = [lax.rem(v + t, n_virt) for t in range(n_virt)]

    small_copies = []
    for i, ref in enumerate((off_hbm, row_hbm, kb_hbm, screen_hbm)):
        c = pltpu.make_async_copy(ref.at[0], small.at[i], small_sem.at[i])
        c.start()
        small_copies.append(c)
    barrier = pltpu.get_barrier_semaphore()
    for o in PEERS:
        pl.semaphore_signal(barrier, inc=1, device_id=(pair_of[o], v), device_id_type=MESH)
    for t in range(1, n_virt):
        pl.semaphore_signal(barrier, inc=1, device_id=(p, virt_of[t]), device_id_type=MESH)

    amp_copies = []
    for j in range(CHUNKS):
        c = pltpu.make_async_copy(amp_hbm.at[0, 0, :, pl.ds(STARTS[j], SIZES[j]), :], amps[j], amp_sem.at[j])
        c.start()
        amp_copies.append(c)
    send_order = (2, 1, 3, 0)
    int_copies = {}
    for t in send_order:
        start = pl.multiple_of(virt_of[t] * cols, cols)
        c = pltpu.make_async_copy(int_hbm.at[0, :, pl.ds(start, cols)], ints.at[t], int_sem.at[t])
        c.start()
        int_copies[t] = c

    gap_copies = [pltpu.make_async_copy(rgap_hbm, rgap, gap_sem.at[0]), pltpu.make_async_copy(cgap_hbm, cgap, gap_sem.at[1])]
    for c in gap_copies:
        c.start()

    none = float(row_count * k_count)
    lane = lax.broadcasted_iota(jnp.int32, (LANES, LANES), 1).astype(jnp.float32)
    sub = lax.broadcasted_iota(jnp.int32, (LANES, LANES), 0).astype(jnp.float32)
    for c in small_copies:
        c.wait()
    rowbuf[...] = jnp.full(rowbuf.shape, -1.0, jnp.float32)
    rowbuf[0:1, 0:slots] = jnp.where(small[3] == 1, small[0], -1).astype(jnp.float32)
    rowbuf[1:2, 0:slots] = (small[1] * k_count + small[2]).astype(jnp.float32)
    want_r = jnp.broadcast_to(rowbuf[0:1, :], (LANES, LANES))
    want_c = want_r.T[:slots]
    blk_c = jnp.broadcast_to(rowbuf[1:2, :], (LANES, LANES)).T[:slots]
    lane_s, sub_s = lane[:slots], sub[:slots]
    rank = jnp.sum(jnp.where((want_r[:slots] == want_c) & (lane_s < sub_s), 1.0, 0.0), axis=1, keepdims=True)
    place = jnp.where(want_c < 0, -1.0, want_c * CAP + rank)
    hit = jnp.where(place == lane_s, 1.0, 0.0)
    slot_of = jnp.sum(hit * sub_s, axis=0, keepdims=True)
    tag_of = none + jnp.sum(hit * (blk_c - none), axis=0, keepdims=True)
    order[0] = jnp.broadcast_to(slot_of.astype(jnp.int32), (8, LANES))
    to_idx = pltpu.make_async_copy(order.at[0], idx_s, idx_sem)
    to_idx.start()
    tag_own[...] = jnp.broadcast_to(tag_of, (8, LANES))
    to_idx.wait()

    def pack_tiles(j, o):
        for s in range(CAP):
            tile = amps[j][jnp.clip(idx_s[0, o * CAP + s], 0, slots - 1)]
            if o == REACH:
                recv[j][o * CAP + s] = tile
            else:
                pack[j][o, s] = tile

    tile_copies = {}

    def send_tiles(j, o):
        c = pltpu.make_async_remote_copy(
            src_ref=pack[j].at[o], dst_ref=recv[j].at[pl.ds(o * CAP, CAP)],
            send_sem=tile_send.at[j, o], recv_sem=tile_recv.at[j, o],
            device_id=(pair_of[o], v), device_id_type=MESH)
        c.start()
        tile_copies[j, o] = c

    amp_copies[0].wait()
    pack_tiles(0, PEERS[0])
    pl.semaphore_wait(barrier, len(PEERS) + n_virt - 1)
    send_tiles(0, PEERS[0])
    for o in PEERS[1:]:
        pack_tiles(0, o)
        send_tiles(0, o)
    tag_copies = []
    for o in PEERS:
        c = pltpu.make_async_remote_copy(
            src_ref=tag_own, dst_ref=tags_in.at[o], send_sem=tag_send.at[o], recv_sem=tag_recv.at[o],
            device_id=(pair_of[o], v), device_id_type=MESH)
        c.start()
        tag_copies.append(c)
    pack_tiles(0, REACH)
    for j in range(1, CHUNKS):
        amp_copies[j].wait()
        for o in PEERS:
            pack_tiles(j, o)
            if j < AHEAD:
                send_tiles(j, o)
        pack_tiles(j, REACH)

    for c in tag_copies:
        c.wait()
    lane8 = lane[:8]
    tag8 = jnp.full((8, LANES), none, jnp.float32)
    for o in range(WINDOW):
        got = tag_own[...] if o == REACH else tags_in[o]
        tag8 = jnp.where((lane8 >= o * CAP) & (lane8 < (o + 1) * CAP), got, tag8)
    tag_r = jnp.broadcast_to(tag8[0:1, :], (LANES, LANES))
    tag_c = tag_r.T
    key_r = tag_r * LANES + lane
    key_c = tag_c * LANES + sub
    rank_c = jnp.sum(jnp.where(key_r < key_c, 1.0, 0.0), axis=1, keepdims=True)
    again_c = jnp.max(jnp.where((tag_r == tag_c) & (lane < sub), 1.0, 0.0), axis=1, keepdims=True)
    here = jnp.where(rank_c == lane, 1.0, 0.0)
    perm = jnp.sum(here * sub, axis=0, keepdims=True)
    again = jnp.sum(here * again_c, axis=0, keepdims=True)
    upto = jnp.sum(jnp.where(tag_c <= lane, 1.0, 0.0), axis=0, keepdims=True)
    equal = jnp.sum(jnp.where(tag_c == lane, 1.0, 0.0), axis=0, keepdims=True)
    last = jnp.where(equal > 0, upto - 1.0, float(CANDS))
    order[1] = jnp.zeros((8, LANES), jnp.int32)
    order[1, 0:1, :] = perm.astype(jnp.int32)
    order[1, 1:2, :] = again.astype(jnp.int32)
    order[1, 2:3, :] = last.astype(jnp.int32)
    to_order = pltpu.make_async_copy(order.at[1], order_s, order_sem)
    to_order.start()
    for c in gap_copies:
        c.wait()
    for r in range(row_count):
        gaps = rgap[pl.ds(r * edge, edge)].reshape(1, edge)
        rowmat[pl.ds(r * edge, edge), :] = jnp.broadcast_to(gaps, (edge, LANES)).T
    for j in range(CHUNKS):
        pref[j][CANDS] = jnp.zeros(pref[j].shape[1:], jnp.bfloat16)
    to_order.wait()

    x_copies = {}

    def finish(j):
        for t in range(1, n_virt):
            x_copies[j, t].wait()
        total = own[j][...]
        for t in range(1, n_virt):
            total = total + xrecv[j][t].astype(jnp.float32)
        rows, col_gap = SIZES[j], cgap[...].reshape(1, cols)
        for r in range(row_count):
            row_gap = rowmat[pl.ds(r * edge + STARTS[j], rows), :]
            gap = jnp.concatenate([row_gap] * (cols // LANES), axis=1) + col_gap
            out_ref[pl.ds(r * edge + STARTS[j], rows), :] = total[r * rows:(r + 1) * rows] / gap

    for j in range(CHUNKS):
        if j + AHEAD < CHUNKS:
            for o in PEERS:
                tile_copies[j, o].wait_send()
            for o in PEERS:
                send_tiles(j + AHEAD, o)
        for o in PEERS:
            tile_copies[j, o].wait_recv()
        rows = SIZES[j]

        acc = jnp.zeros((rows, LANES), jnp.float32)
        for at in range(CANDS):
            tile = recv[j][jnp.clip(order_s[0, at], 0, CANDS - 1)].astype(jnp.float32)
            acc = jnp.where(order_s[1, at] > 0, acc, 0.0) + tile
            pref[j][at] = acc.astype(jnp.bfloat16)
        for r in range(row_count):
            for k in range(k_count):
                block = pref[j][jnp.clip(order_s[2, r * k_count + k], 0, CANDS)]
                assembled[j][pl.ds(r * rows, rows), pl.ds(k * LANES, LANES)] = block
        for t in send_order:
            if j == 0:
                int_copies[t].wait()
            part = jnp.dot(assembled[j][...], ints[t], preferred_element_type=jnp.float32)
            if t == 0:
                own[j][...] = part
            else:
                xsend[j][t] = part.astype(jnp.bfloat16)
                c = pltpu.make_async_remote_copy(
                    src_ref=xsend[j].at[t], dst_ref=xrecv[j].at[t], send_sem=x_send.at[j, t], recv_sem=x_recv.at[j, t],
                    device_id=(p, virt_of[t]), device_id_type=MESH)
                c.start()
                x_copies[j, t] = c
        if j >= LAG:
            finish(j - LAG)
    for j in range(max(0, CHUNKS - AHEAD), CHUNKS):
        for o in PEERS:
            tile_copies[j, o].wait_send()
    for j in range(max(0, CHUNKS - LAG), CHUNKS):
        finish(j)


def on_device(n_pair, n_virt, amplitudes, offsets, row_blocks, k_blocks, screen, integrals, row_gaps, col_gaps):
    slots, edge = amplitudes.shape[2], amplitudes.shape[3]
    k_count = integrals.shape[1] // edge
    row_count = row_gaps.shape[0] // edge
    cols = col_gaps.shape[0]

    def chunked(shape_of, dtype):
        return [pltpu.VMEM(shape_of(rows), dtype) for rows in SIZES]

    operands = (offsets[..., 0], row_blocks, k_blocks, screen, amplitudes, integrals, row_gaps, col_gaps)
    return pl.pallas_call(
        functools.partial(kernel, n_pair, n_virt, row_count, k_count),
        out_shape=jax.ShapeDtypeStruct((row_count * edge, cols), jnp.float32),
        in_specs=[pl.BlockSpec(memory_space=pltpu.HBM)] * 8,
        out_specs=pl.BlockSpec(memory_space=pltpu.VMEM),
        scratch_shapes=[
            chunked(lambda rows: (slots, rows, edge), jnp.bfloat16),
            chunked(lambda rows: (WINDOW, CAP, rows, edge), jnp.bfloat16),
            chunked(lambda rows: (CANDS, rows, edge), jnp.bfloat16),
            chunked(lambda rows: (CANDS + 1, rows, edge), jnp.bfloat16),
            chunked(lambda rows: (row_count * rows, k_count * edge), jnp.bfloat16),
            chunked(lambda rows: (row_count * rows, cols), jnp.float32),
            chunked(lambda rows: (n_virt, row_count * rows, cols), jnp.bfloat16),
            chunked(lambda rows: (n_virt, row_count * rows, cols), jnp.bfloat16),
            pltpu.VMEM((n_virt, k_count * edge, cols), jnp.bfloat16),
            pltpu.VMEM((WINDOW, 8, LANES), jnp.float32),
            pltpu.VMEM((8, LANES), jnp.float32),
            pltpu.VMEM((8, LANES), jnp.float32),
            pltpu.VMEM((4, 1, slots), jnp.int32),
            pltpu.VMEM((row_count * edge,), jnp.float32),
            pltpu.VMEM((cols,), jnp.float32),
            pltpu.VMEM((row_count * edge, LANES), jnp.float32),
            pltpu.VMEM((2, 8, LANES), jnp.int32),
            pltpu.SMEM((8, LANES), jnp.int32),
            pltpu.SMEM((8, LANES), jnp.int32),
            pltpu.SemaphoreType.DMA((CHUNKS,)),
            pltpu.SemaphoreType.DMA((n_virt,)),
            pltpu.SemaphoreType.DMA((4,)),
            pltpu.SemaphoreType.DMA((2,)),
            pltpu.SemaphoreType.DMA,
            pltpu.SemaphoreType.DMA,
            pltpu.SemaphoreType.DMA((WINDOW,)),
            pltpu.SemaphoreType.DMA((WINDOW,)),
            pltpu.SemaphoreType.DMA((CHUNKS, WINDOW)),
            pltpu.SemaphoreType.DMA((CHUNKS, WINDOW)),
            pltpu.SemaphoreType.DMA((CHUNKS, n_virt)),
            pltpu.SemaphoreType.DMA((CHUNKS, n_virt)),
        ],
        compiler_params=pltpu.CompilerParams(
            collective_id=0, has_side_effects=True, vmem_limit_bytes=40 * 1024 * 1024),
        name="cycle",
    )(*[pltpu.with_memory_space_constraint(x, pltpu.HBM) for x in operands])


def solution(mesh):
    return jax.shard_map(
        functools.partial(on_device, mesh.shape["pair"], mesh.shape["virt"]),
        mesh=mesh,
        in_specs=(
            P("pair", "virt", None, None, None),
            P("pair", "virt", None, None),
            P("pair", "virt", None),
            P("pair", "virt", None),
            P("pair", "virt", None),
            P("pair", "virt", None),
            P("pair"),
            P("virt"),
        ),
        out_specs=P("pair", "virt"),
        check_vma=False,
    )
```

time: 48.9 us -> 43.3 us (0.89)
  other arithmetic: 4.12 us -> 0 us
  Pallas kernels: 43.9 us -> 42.3 us
    div x1 -> x0, other arithmetic: 1.98 us -> none  [on_device(): return cycle / (row_gaps[:, None] + col_gaps[None, :])]
    pallas_call x1, Pallas kernels: 43.9 us -> 42.3 us  [on_device(): pl.pallas_call(functools.partial(kernel, n_pair, n_virt, row_count, k_cou...]
    unnamed x4 -> x1, local copies, waits for them, and re-layouts: 0.01 us -> 0.8 us
    reduce_sum x2 -> x0, other arithmetic: 0.78 us -> none  [the longest x1 0.69 us: on_device(): tag = none + jnp.sum(jnp.where(hit, blk[None, :] - none, 0), axis=1)]
    select_n x2 -> x0, other arithmetic: 0.68 us -> none  [the longest x1 0.67 us: on_device(): wanted = jnp.where(screen[0, 0] == 1, off, -1)]
    sub x1 -> x0, other arithmetic: 0.68 us -> none  [on_device(): tag = none + jnp.sum(jnp.where(hit, blk[None, :] - none, 0), axis=1)]
    broadcast_in_dim x1 -> x0, local copies, waits for them, and re-layouts: 0.6 us -> none  [on_device(): tag = jnp.broadcast_to(tag[None, :], (8, LANES))]
where the time goes in v2:
time: 43.3 us; the launch traced here: 43.1 us
  Pallas kernels  42.3 us (98%)
  local copies, waits for them, and re-layouts  0.8 us (2%)
    pallas_call x1, Pallas kernels, on_device(): pl.pallas_call(functools.partial(kernel, n_pair, n_virt, row_count, k_cou...  42.3 us

profile of v2, /device:TPU:1, one launch (start us, length us, event | category | flops | bytes accessed | tf_op | source)
XLA Modules:
  0.0 43.1 jit_solution(1037840673102018295)
XLA Ops:
  0.0 42.3 %cycle.1 = f32[512,256]{1,0:T(8,128)S(1)} custom-call(s32[1,1,48]{2,1,0:T(1,128)} %bitcast.1, s32[1,1,48]{2,1,0:T(1,128)} %row_hbm.1, s32[1,1,48]{2,1,0:T(1,128)} %kb_hbm.1, s32[1,1,48]{2,1,0:T(1,128)} %screen_hbm.1, bf16[1,1,48,128,128]{4,3,2,1,0:T(8,128)(2,1)} %amp_hbm.1, bf16[1,1024,1024]{2,1,0:T(8,128)(2,1)} %int_hbm.1, f32[512]{0:T(512)} %rgap_hbm.1, ...), custom_call_target="tpu_custom_call" | custom-call | tf_op jit(solution)/shard_map/cycle/pallas_call | solution.py:224
  42.3 0.8 %copy.10 = f32[512,256]{1,0:T(8,128)} copy(f32[512,256]{1,0:T(8,128)S(1)} %cycle.1) | data formatting | bytes 1048576

commit v3 on v2

--- a/solution.py
+++ b/solution.py
@@ -18,11 +18,20 @@
 LAG = 2
 MESH = pl.DeviceIdType.MESH
 PEERS = (4, 3, 1, 0)
+REMOTE = (WINDOW - 1) * CAP
+
+
+def place_of(o):
+    return WINDOW - 1 if o == REACH else o - (o > REACH)
+
+
+def wait_bytes(ref, sem):
+    pltpu.make_async_copy(ref, ref, sem).wait()
 
 
 def kernel(n_pair, n_virt, row_count, k_count, off_hbm, row_hbm, kb_hbm, screen_hbm, amp_hbm, int_hbm, rgap_hbm, cgap_hbm, out_ref,
-           amps, pack, recv, pref, assembled, own, xsend, xrecv, ints, tags_in, tag_own, rowbuf, small, rgap, cgap, rowmat, order, idx_s, order_s,
-           amp_sem, int_sem, small_sem, gap_sem, idx_sem, order_sem, tag_send, tag_recv, tile_send, tile_recv, x_send, x_recv):
+           amp_first, amp_rest, pack, recv, pref, assembled, own, xsend, xrecv, ints, tags_in, tag_own, rowbuf, small, rgap, cgap, rowmat, order, idx_s, order_s,
+           amp_sem, int_sem, small_sem, gap_sem, order_sem, tag_send, tag_recv, tile_send, tile_recv, x_send, x_recv):
     p = lax.axis_index("pair")
     v = lax.axis_index("virt")
     slots, edge = amp_hbm.shape[2:4]
@@ -41,19 +50,15 @@
     for t in range(1, n_virt):
         pl.semaphore_signal(barrier, inc=1, device_id=(p, virt_of[t]), device_id_type=MESH)
 
-    amp_copies = []
-    for j in range(CHUNKS):
-        c = pltpu.make_async_copy(amp_hbm.at[0, 0, :, pl.ds(STARTS[j], SIZES[j]), :], amps[j], amp_sem.at[j])
+    first = SIZES[0]
+    amp_copies = [
+        pltpu.make_async_copy(amp_hbm.at[0, 0, :, pl.ds(0, first), :], amp_first, amp_sem.at[0]),
+        pltpu.make_async_copy(amp_hbm.at[0, 0, :, pl.ds(first, edge - first), :], amp_rest, amp_sem.at[1]),
+    ]
+    int_copy = pltpu.make_async_copy(int_hbm.at[0], ints, int_sem)
+    for c in amp_copies:
         c.start()
-        amp_copies.append(c)
-    send_order = (2, 1, 3, 0)
-    int_copies = {}
-    for t in send_order:
-        start = pl.multiple_of(virt_of[t] * cols, cols)
-        c = pltpu.make_async_copy(int_hbm.at[0, :, pl.ds(start, cols)], ints.at[t], int_sem.at[t])
-        c.start()
-        int_copies[t] = c
-
+    int_copy.start()
     gap_copies = [pltpu.make_async_copy(rgap_hbm, rgap, gap_sem.at[0]), pltpu.make_async_copy(cgap_hbm, cgap, gap_sem.at[1])]
     for c in gap_copies:
         c.start()
@@ -71,33 +76,31 @@
     blk_c = jnp.broadcast_to(rowbuf[1:2, :], (LANES, LANES)).T[:slots]
     lane_s, sub_s = lane[:slots], sub[:slots]
     rank = jnp.sum(jnp.where((want_r[:slots] == want_c) & (lane_s < sub_s), 1.0, 0.0), axis=1, keepdims=True)
-    place = jnp.where(want_c < 0, -1.0, want_c * CAP + rank)
+    position = jnp.where(want_c > REACH, want_c - 1, jnp.where(want_c == REACH, float(WINDOW - 1), want_c))
+    place = jnp.where(want_c < 0, -1.0, position * CAP + rank)
     hit = jnp.where(place == lane_s, 1.0, 0.0)
     slot_of = jnp.sum(hit * sub_s, axis=0, keepdims=True)
     tag_of = none + jnp.sum(hit * (blk_c - none), axis=0, keepdims=True)
     order[0] = jnp.broadcast_to(slot_of.astype(jnp.int32), (8, LANES))
-    to_idx = pltpu.make_async_copy(order.at[0], idx_s, idx_sem)
+    to_idx = pltpu.make_async_copy(order.at[0], idx_s, order_sem)
     to_idx.start()
     tag_own[...] = jnp.broadcast_to(tag_of, (8, LANES))
     to_idx.wait()
 
     def pack_tiles(j, o):
         for s in range(CAP):
-            tile = amps[j][jnp.clip(idx_s[0, o * CAP + s], 0, slots - 1)]
+            slot = jnp.clip(idx_s[0, place_of(o) * CAP + s], 0, slots - 1)
+            tile = amp_first[slot] if j == 0 else amp_rest[slot, pl.ds(STARTS[j] - first, SIZES[j]), :]
             if o == REACH:
-                recv[j][o * CAP + s] = tile
+                recv[j][REMOTE + s] = tile
             else:
-                pack[j][o, s] = tile
-
-    tile_copies = {}
+                pack[j][place_of(o) * CAP + s] = tile
 
     def send_tiles(j, o):
-        c = pltpu.make_async_remote_copy(
-            src_ref=pack[j].at[o], dst_ref=recv[j].at[pl.ds(o * CAP, CAP)],
-            send_sem=tile_send.at[j, o], recv_sem=tile_recv.at[j, o],
-            device_id=(pair_of[o], v), device_id_type=MESH)
-        c.start()
-        tile_copies[j, o] = c
+        there = pl.ds(place_of(o) * CAP, CAP)
+        pltpu.make_async_remote_copy(
+            src_ref=pack[j].at[there], dst_ref=recv[j].at[there], send_sem=tile_send.at[j], recv_sem=tile_recv.at[j],
+            device_id=(pair_of[o], v), device_id_type=MESH).start()
 
     amp_copies[0].wait()
     pack_tiles(0, PEERS[0])
@@ -106,28 +109,25 @@
     for o in PEERS[1:]:
         pack_tiles(0, o)
         send_tiles(0, o)
-    tag_copies = []
     for o in PEERS:
-        c = pltpu.make_async_remote_copy(
-            src_ref=tag_own, dst_ref=tags_in.at[o], send_sem=tag_send.at[o], recv_sem=tag_recv.at[o],
-            device_id=(pair_of[o], v), device_id_type=MESH)
-        c.start()
-        tag_copies.append(c)
+        pltpu.make_async_remote_copy(
+            src_ref=tag_own, dst_ref=tags_in.at[place_of(o)], send_sem=tag_send, recv_sem=tag_recv,
+            device_id=(pair_of[o], v), device_id_type=MESH).start()
     pack_tiles(0, REACH)
+    amp_copies[1].wait()
     for j in range(1, CHUNKS):
-        amp_copies[j].wait()
         for o in PEERS:
             pack_tiles(j, o)
             if j < AHEAD:
                 send_tiles(j, o)
         pack_tiles(j, REACH)
 
-    for c in tag_copies:
-        c.wait()
+    wait_bytes(tags_in, tag_recv)
+    wait_bytes(tags_in, tag_send)
     lane8 = lane[:8]
     tag8 = jnp.full((8, LANES), none, jnp.float32)
     for o in range(WINDOW):
-        got = tag_own[...] if o == REACH else tags_in[o]
+        got = tag_own[...] if o == WINDOW - 1 else tags_in[o]
         tag8 = jnp.where((lane8 >= o * CAP) & (lane8 < (o + 1) * CAP), got, tag8)
     tag_r = jnp.broadcast_to(tag8[0:1, :], (LANES, LANES))
     tag_c = tag_r.T
@@ -156,28 +156,25 @@
         pref[j][CANDS] = jnp.zeros(pref[j].shape[1:], jnp.bfloat16)
     to_order.wait()
 
-    x_copies = {}
-
     def finish(j):
-        for t in range(1, n_virt):
-            x_copies[j, t].wait()
+        wait_bytes(xsend[j], x_send.at[j])
+        wait_bytes(xrecv[j], x_recv.at[j])
         total = own[j][...]
         for t in range(1, n_virt):
-            total = total + xrecv[j][t].astype(jnp.float32)
+            total = total + xrecv[j][t - 1].astype(jnp.float32)
         rows, col_gap = SIZES[j], cgap[...].reshape(1, cols)
         for r in range(row_count):
             row_gap = rowmat[pl.ds(r * edge + STARTS[j], rows), :]
             gap = jnp.concatenate([row_gap] * (cols // LANES), axis=1) + col_gap
             out_ref[pl.ds(r * edge + STARTS[j], rows), :] = total[r * rows:(r + 1) * rows] / gap
 
+    send_order = (2, 1, 3, 0)
     for j in range(CHUNKS):
         if j + AHEAD < CHUNKS:
-            for o in PEERS:
-                tile_copies[j, o].wait_send()
+            wait_bytes(pack[j], tile_send.at[j])
             for o in PEERS:
                 send_tiles(j + AHEAD, o)
-        for o in PEERS:
-            tile_copies[j, o].wait_recv()
+        wait_bytes(recv[j].at[pl.ds(0, REMOTE)], tile_recv.at[j])
         rows = SIZES[j]
 
         acc = jnp.zeros((rows, LANES), jnp.float32)
@@ -190,23 +187,21 @@
                 block = pref[j][jnp.clip(order_s[2, r * k_count + k], 0, CANDS)]
                 assembled[j][pl.ds(r * rows, rows), pl.ds(k * LANES, LANES)] = block
         for t in send_order:
-            if j == 0:
-                int_copies[t].wait()
-            part = jnp.dot(assembled[j][...], ints[t], preferred_element_type=jnp.float32)
+            if j == 0 and t == send_order[0]:
+                int_copy.wait()
+            columns = pl.ds(pl.multiple_of(virt_of[t] * cols, cols), cols)
+            part = jnp.dot(assembled[j][...], ints[:, columns], preferred_element_type=jnp.float32)
             if t == 0:
                 own[j][...] = part
             else:
-                xsend[j][t] = part.astype(jnp.bfloat16)
-                c = pltpu.make_async_remote_copy(
-                    src_ref=xsend[j].at[t], dst_ref=xrecv[j].at[t], send_sem=x_send.at[j, t], recv_sem=x_recv.at[j, t],
-                    device_id=(p, virt_of[t]), device_id_type=MESH)
-                c.start()
-                x_copies[j, t] = c
+                xsend[j][t - 1] = part.astype(jnp.bfloat16)
+                pltpu.make_async_remote_copy(
+                    src_ref=xsend[j].at[t - 1], dst_ref=xrecv[j].at[t - 1], send_sem=x_send.at[j], recv_sem=x_recv.at[j],
+                    device_id=(p, virt_of[t]), device_id_type=MESH).start()
         if j >= LAG:
             finish(j - LAG)
     for j in range(max(0, CHUNKS - AHEAD), CHUNKS):
-        for o in PEERS:
-            tile_copies[j, o].wait_send()
+        wait_bytes(pack[j], tile_send.at[j])
     for j in range(max(0, CHUNKS - LAG), CHUNKS):
         finish(j)
 
@@ -227,16 +222,17 @@
         in_specs=[pl.BlockSpec(memory_space=pltpu.HBM)] * 8,
         out_specs=pl.BlockSpec(memory_space=pltpu.VMEM),
         scratch_shapes=[
-            chunked(lambda rows: (slots, rows, edge), jnp.bfloat16),
-            chunked(lambda rows: (WINDOW, CAP, rows, edge), jnp.bfloat16),
+            pltpu.VMEM((slots, SIZES[0], edge), jnp.bfloat16),
+            pltpu.VMEM((slots, edge - SIZES[0], edge), jnp.bfloat16),
+            chunked(lambda rows: (REMOTE, rows, edge), jnp.bfloat16),
             chunked(lambda rows: (CANDS, rows, edge), jnp.bfloat16),
             chunked(lambda rows: (CANDS + 1, rows, edge), jnp.bfloat16),
             chunked(lambda rows: (row_count * rows, k_count * edge), jnp.bfloat16),
             chunked(lambda rows: (row_count * rows, cols), jnp.float32),
-            chunked(lambda rows: (n_virt, row_count * rows, cols), jnp.bfloat16),
-            chunked(lambda rows: (n_virt, row_count * rows, cols), jnp.bfloat16),
-            pltpu.VMEM((n_virt, k_count * edge, cols), jnp.bfloat16),
-            pltpu.VMEM((WINDOW, 8, LANES), jnp.float32),
+            chunked(lambda rows: (n_virt - 1, row_count * rows, cols), jnp.bfloat16),
+            chunked(lambda rows: (n_virt - 1, row_count * rows, cols), jnp.bfloat16),
+            pltpu.VMEM((k_count * edge, n_virt * cols), jnp.bfloat16),
+            pltpu.VMEM((WINDOW - 1, 8, LANES), jnp.float32),
             pltpu.VMEM((8, LANES), jnp.float32),
             pltpu.VMEM((8, LANES), jnp.float32),
             pltpu.VMEM((4, 1, slots), jnp.int32),
@@ -246,18 +242,17 @@
             pltpu.VMEM((2, 8, LANES), jnp.int32),
             pltpu.SMEM((8, LANES), jnp.int32),
             pltpu.SMEM((8, LANES), jnp.int32),
-            pltpu.SemaphoreType.DMA((CHUNKS,)),
-            pltpu.SemaphoreType.DMA((n_virt,)),
+            pltpu.SemaphoreType.DMA((2,)),
+            pltpu.SemaphoreType.DMA,
             pltpu.SemaphoreType.DMA((4,)),
             pltpu.SemaphoreType.DMA((2,)),
             pltpu.SemaphoreType.DMA,
             pltpu.SemaphoreType.DMA,
-            pltpu.SemaphoreType.DMA((WINDOW,)),
-            pltpu.SemaphoreType.DMA((WINDOW,)),
-            pltpu.SemaphoreType.DMA((CHUNKS, WINDOW)),
-            pltpu.SemaphoreType.DMA((CHUNKS, WINDOW)),
-            pltpu.SemaphoreType.DMA((CHUNKS, n_virt)),
-            pltpu.SemaphoreType.DMA((CHUNKS, n_virt)),
+            pltpu.SemaphoreType.DMA,
+            pltpu.SemaphoreType.DMA((CHUNKS,)),
+            pltpu.SemaphoreType.DMA((CHUNKS,)),
+            pltpu.SemaphoreType.DMA((CHUNKS,)),
+            pltpu.SemaphoreType.DMA((CHUNKS,)),
         ],
         compiler_params=pltpu.CompilerParams(
             collective_id=0, has_side_effects=True, vmem_limit_bytes=40 * 1024 * 1024),

time: 43.3 us -> 42.5 us (0.982)
  Pallas kernels: 42.3 us -> 41.6 us
    pallas_call x1, Pallas kernels: 42.3 us -> 41.6 us  [on_device(): pl.pallas_call(functools.partial(kernel, n_pair, n_virt, row_count, k_cou...]
where the time goes in v3:
time: 42.5 us; the launch traced here: 42.4 us
  Pallas kernels  41.6 us (98%)
  local copies, waits for them, and re-layouts  0.8 us (2%)
    pallas_call x1, Pallas kernels, on_device(): pl.pallas_call(functools.partial(kernel, n_pair, n_virt, row_count, k_cou...  41.6 us

profile of v3, /device:TPU:1, one launch (start us, length us, event | category | flops | bytes accessed | tf_op | source)
XLA Modules:
  0.0 42.4 jit_solution(11352770852855396898)
XLA Ops:
  0.0 41.6 %cycle.1 = f32[512,256]{1,0:T(8,128)S(1)} custom-call(s32[1,1,48]{2,1,0:T(1,128)} %bitcast.1, s32[1,1,48]{2,1,0:T(1,128)} %row_hbm.1, s32[1,1,48]{2,1,0:T(1,128)} %kb_hbm.1, s32[1,1,48]{2,1,0:T(1,128)} %screen_hbm.1, bf16[1,1,48,128,128]{4,3,2,1,0:T(8,128)(2,1)} %amp_hbm.1, bf16[1,1024,1024]{2,1,0:T(8,128)(2,1)} %int_hbm.1, f32[512]{0:T(512)} %rgap_hbm.1, ...), custom_call_target="tpu_custom_call" | custom-call | tf_op jit(solution)/shard_map/cycle/pallas_call | solution.py:219
  41.6 0.8 %copy.10 = f32[512,256]{1,0:T(8,128)} copy(f32[512,256]{1,0:T(8,128)S(1)} %cycle.1) | data formatting | bytes 1048576

commit v4 on v3

--- a/solution.py
+++ b/solution.py
@@ -56,12 +56,8 @@
         pltpu.make_async_copy(amp_hbm.at[0, 0, :, pl.ds(first, edge - first), :], amp_rest, amp_sem.at[1]),
     ]
     int_copy = pltpu.make_async_copy(int_hbm.at[0], ints, int_sem)
-    for c in amp_copies:
-        c.start()
-    int_copy.start()
+    amp_copies[0].start()
     gap_copies = [pltpu.make_async_copy(rgap_hbm, rgap, gap_sem.at[0]), pltpu.make_async_copy(cgap_hbm, cgap, gap_sem.at[1])]
-    for c in gap_copies:
-        c.start()
 
     none = float(row_count * k_count)
     lane = lax.broadcasted_iota(jnp.int32, (LANES, LANES), 1).astype(jnp.float32)
@@ -80,12 +76,16 @@
     place = jnp.where(want_c < 0, -1.0, position * CAP + rank)
     hit = jnp.where(place == lane_s, 1.0, 0.0)
     slot_of = jnp.sum(hit * sub_s, axis=0, keepdims=True)
-    tag_of = none + jnp.sum(hit * (blk_c - none), axis=0, keepdims=True)
     order[0] = jnp.broadcast_to(slot_of.astype(jnp.int32), (8, LANES))
     to_idx = pltpu.make_async_copy(order.at[0], idx_s, order_sem)
     to_idx.start()
+    tag_of = none + jnp.sum(hit * (blk_c - none), axis=0, keepdims=True)
     tag_own[...] = jnp.broadcast_to(tag_of, (8, LANES))
     to_idx.wait()
+    amp_copies[1].start()
+    int_copy.start()
+    for c in gap_copies:
+        c.start()
 
     def pack_tiles(j, o):
         for s in range(CAP):
@@ -157,7 +157,6 @@
     to_order.wait()
 
     def finish(j):
-        wait_bytes(xsend[j], x_send.at[j])
         wait_bytes(xrecv[j], x_recv.at[j])
         total = own[j][...]
         for t in range(1, n_virt):
@@ -168,7 +167,7 @@
             gap = jnp.concatenate([row_gap] * (cols // LANES), axis=1) + col_gap
             out_ref[pl.ds(r * edge + STARTS[j], rows), :] = total[r * rows:(r + 1) * rows] / gap
 
-    send_order = (2, 1, 3, 0)
+    send_order = (1, 3, 2, 0)
     for j in range(CHUNKS):
         if j + AHEAD < CHUNKS:
             wait_bytes(pack[j], tile_send.at[j])
@@ -200,10 +199,12 @@
                     device_id=(p, virt_of[t]), device_id_type=MESH).start()
         if j >= LAG:
             finish(j - LAG)
+    for j in range(max(0, CHUNKS - LAG), CHUNKS):
+        finish(j)
     for j in range(max(0, CHUNKS - AHEAD), CHUNKS):
         wait_bytes(pack[j], tile_send.at[j])
-    for j in range(max(0, CHUNKS - LAG), CHUNKS):
-        finish(j)
+    for j in range(CHUNKS):
+        wait_bytes(xsend[j], x_send.at[j])
 
 
 def on_device(n_pair, n_virt, amplitudes, offsets, row_blocks, k_blocks, screen, integrals, row_gaps, col_gaps):

time: 42.5 us -> 42.4 us (level)
  no operation moved by 1% of the time
where the time goes in v4:
time: 42.4 us; the launch traced here: 42.3 us
  Pallas kernels  41.5 us (98%)
  local copies, waits for them, and re-layouts  0.8 us (2%)
    pallas_call x1, Pallas kernels, on_device(): pl.pallas_call(functools.partial(kernel, n_pair, n_virt, row_count, k_cou...  41.5 us

profile of v4, /device:TPU:1, one launch (start us, length us, event | category | flops | bytes accessed | tf_op | source)
XLA Modules:
  0.0 42.3 jit_solution(2676365231344977833)
XLA Ops:
  0.0 41.5 %cycle.1 = f32[512,256]{1,0:T(8,128)S(1)} custom-call(s32[1,1,48]{2,1,0:T(1,128)} %bitcast.1, s32[1,1,48]{2,1,0:T(1,128)} %row_hbm.1, s32[1,1,48]{2,1,0:T(1,128)} %kb_hbm.1, s32[1,1,48]{2,1,0:T(1,128)} %screen_hbm.1, bf16[1,1,48,128,128]{4,3,2,1,0:T(8,128)(2,1)} %amp_hbm.1, bf16[1,1024,1024]{2,1,0:T(8,128)(2,1)} %int_hbm.1, f32[512]{0:T(512)} %rgap_hbm.1, ...), custom_call_target="tpu_custom_call" | custom-call | tf_op jit(solution)/shard_map/cycle/pallas_call | solution.py:220
  41.5 0.8 %copy.10 = f32[512,256]{1,0:T(8,128)} copy(f32[512,256]{1,0:T(8,128)S(1)} %cycle.1) | data formatting | bytes 1048576
